TPU v7x, 1024 devices: a whole 8x8x8 slice. The times are simulated.
1024 devices in a mesh: gx: 32 (over x_hi, y, core), gy: 4 (over x_lo), gz: 8 (over z).
Axes of the slice: x: 8 (x_hi: 2, x_lo: 4; x = x_hi * 4 + x_lo), y: 8, z: 8, core: 2. Of those that a mesh axis runs over, the one named last changes fastest.
Arguments:
- offsets: float32 [64, 8, 16, 3, 128], P('gx', 'gy', 'gz'), may hold values from 0 to 1
- velocity: float32 [64, 8, 16, 3, 128], P('gx', 'gy', 'gz'), may hold values from -6 to 6
- mass: float32 [64, 8, 16, 128], P('gx', 'gy', 'gz'), may hold values from 0.05 to 0.2
- energy: float32 [64, 8, 16, 128], P('gx', 'gy', 'gz'), may hold values from 0.5 to 2
- partner_mask: int32 [64, 8, 16, 27], P('gx', 'gy', 'gz'), may hold values from 0 to 1, as said below
- counts: int32 [64, 8, 16], P('gx', 'gy', 'gz'), may hold values from 1 to 128, as said below
Outputs:
- acceleration: float32 [64, 8, 16, 3, 128], P('gx', 'gy', 'gz')
- energy_rate: float32 [64, 8, 16, 128], P('gx', 'gy', 'gz')
Inputs may be any that keep to these rules, and one draw needn't show every extreme that they name: `partner_mask`: partner 13 (the leaf itself) is always 1. `counts`: some leaf holds 128 valid particles.
All inputs are finite; a program needn't handle non-finite values.
Results may differ from a plain program's by a relative error of at most 0.0003.
Values sent between devices are 32-bit elements; how exact they have to be, the bound alone decides.
A program may use at most 32 MiB of HBM per device.

v0:
```python
import jax
import jax.numpy as jnp
from jax import lax
from jax.sharding import PartitionSpec as P


def extended(block, sides, width):
    for axis, dim in sides:
        count = lax.axis_size(axis)
        forward = [(i, i + 1) for i in range(count - 1)]
        forward.append((count - 1, 0))
        backward = [(target, source) for source, target in forward]
        low = lax.ppermute(
            lax.slice_in_dim(block, block.shape[dim] - width, None, axis=dim), axis, forward
        )
        high = lax.ppermute(lax.slice_in_dim(block, 0, width, axis=dim), axis, backward)
        block = jnp.concatenate([low, block, high], axis=dim)
    return block


def pair_geometry(center, partner, shift):
    separation = (
        center[:, :, 0:3, :, None] - partner[:, :, 0:3, None, :] - shift[None, None, :, None, None]
    )
    radius = jnp.sqrt(jnp.sum(separation * separation, axis=2))
    inside = jnp.maximum(1.0 - radius, 0.0)
    cubed = inside * inside * inside
    kernel = cubed * inside * (1.0 + 4.0 * radius)
    slope = -20.0 * cubed
    return (separation, kernel, slope)


def volume_terms(center, partner, shift):
    separation, kernel, slope = pair_geometry(center, partner, shift)
    return jnp.sum(kernel * partner[:, :, 3, None, :], axis=-1)[:, :, None, :]


def density_terms(center, partner, shift):
    separation, kernel, slope = pair_geometry(center, partner, shift)
    weight = partner[:, :, 3, None, :]
    mass_far = partner[:, :, 4, None, :]
    volume_far = partner[:, :, 8, None, :]
    summed_mass = jnp.sum(weight * mass_far * kernel, axis=-1)
    summed_volume = jnp.sum(weight * volume_far * kernel, axis=-1)
    relative = jnp.sum(
        (partner[:, :, 5:8, None, :] - center[:, :, 5:8, :, None]) * separation, axis=2
    )
    divergence = jnp.sum(weight * volume_far * slope * relative, axis=-1)
    return jnp.stack([summed_mass, summed_volume, divergence], axis=2)


def force_terms(center, partner, shift):
    separation, kernel, slope = pair_geometry(center, partner, shift)
    weight = partner[:, :, 3, None, :]
    mass_far = partner[:, :, 4, None, :]
    dens_own = center[:, :, 9, :, None]
    dens_far = partner[:, :, 9, None, :]
    specific_own = center[:, :, 10, :, None] / (dens_own * dens_own)
    specific_far = partner[:, :, 10, None, :] / (dens_far * dens_far)
    visc_own = jnp.maximum(-center[:, :, 11, :, None], 0.0)
    visc_far = jnp.maximum(-partner[:, :, 11, None, :], 0.0)
    damping = 2.0 * (visc_own + visc_far) / (dens_own + dens_far)
    scaled = weight * mass_far * slope
    push = scaled * (specific_own + specific_far + damping)
    accel = -jnp.sum(push[:, :, None] * separation, axis=-1)
    closing = jnp.sum(
        (center[:, :, 5:8, :, None] - partner[:, :, 5:8, None, :]) * separation, axis=2
    )
    heating = jnp.sum(scaled * (specific_own + 0.5 * damping) * closing, axis=-1)
    return jnp.concatenate([accel, heating[:, :, None, :]], axis=2)


def sweep(padded, mask, terms_fn, width_out):
    rows = padded.shape[0] - 2
    cols = padded.shape[1] - 2
    depth = padded.shape[2] - 2
    chans = padded.shape[3]
    slots = padded.shape[4]
    zero = jnp.zeros((), jnp.int32)

    def leaf_row(index):
        slab = lax.dynamic_slice_in_dim(padded, index, 3, 0)
        center = slab[1, 1:-1, 1:-1]
        row_mask = None
        if mask is not None:
            row_mask = lax.dynamic_index_in_dim(mask, index, 0, keepdims=False).astype(jnp.float32)

        def partner_step(partner, total):
            off_x = partner // 9
            off_y = partner // 3 % 3
            off_z = partner % 3
            neighbour = lax.dynamic_slice(
                slab, (off_x, off_y, off_z, zero, zero), (1, cols, depth, chans, slots)
            )[0]
            shift = jnp.stack([off_x, off_y, off_z]).astype(jnp.float32) - 1.0
            terms = terms_fn(center, neighbour, shift)
            if row_mask is not None:
                picked = lax.dynamic_index_in_dim(row_mask, partner, 2, keepdims=False)
                terms = terms * picked[:, :, None, None]
            return total + terms

        start = jnp.zeros((cols, depth, width_out, slots), jnp.float32)
        return lax.fori_loop(jnp.int32(0), jnp.int32(27), partner_step, start)

    return lax.map(leaf_row, jnp.arange(rows, dtype=jnp.int32))


def shards(offsets, velocity, mass, energy, partner_mask, counts):
    slots = offsets.shape[4]
    slot_ids = jnp.arange(slots, dtype=jnp.int32)
    valid = (slot_ids[None, None, None, :] < counts[:, :, :, None]).astype(jnp.float32)
    base = jnp.concatenate([offsets, valid[:, :, :, None], mass[:, :, :, None], velocity], axis=3)
    nearby = extended(base[:, :, :, 0:4], (("gx", 0), ("gy", 1), ("gz", 2)), 1)
    volume = 1.0 / (1.0 + sweep(nearby, None, volume_terms, 1)[:, :, :, 0])
    carried = jnp.concatenate([base[:, :, :, 4:8], volume[:, :, :, None]], axis=3)
    carried_pad = extended(carried, (("gx", 0), ("gy", 1), ("gz", 2)), 1)
    second_pad = jnp.concatenate([nearby, carried_pad], axis=3)
    summed = sweep(second_pad, partner_mask, density_terms, 3)
    density = (mass + summed[:, :, :, 0]) / (volume + summed[:, :, :, 1])
    divergence = summed[:, :, :, 2]
    pressure = 2.0 / 3.0 * density * energy
    state = jnp.stack([density, pressure, divergence], axis=3)
    state_pad = extended(state, (("gx", 0), ("gy", 1), ("gz", 2)), 1)
    third = jnp.concatenate([second_pad, state_pad], axis=3)
    forces = sweep(third, partner_mask, force_terms, 4)
    acceleration = forces[:, :, :, 0:3] * valid[:, :, :, None]
    energy_rate = forces[:, :, :, 3] * valid
    return (acceleration, energy_rate)


def solution(mesh):
    placed = (
        P("gx", "gy", "gz", None, None),
        P("gx", "gy", "gz", None, None),
        P("gx", "gy", "gz", None),
        P("gx", "gy", "gz", None),
        P("gx", "gy", "gz", None),
        P("gx", "gy", "gz"),
    )
    return jax.shard_map(
        shards,
        mesh=mesh,
        in_specs=placed,
        out_specs=(P("gx", "gy", "gz", None, None), P("gx", "gy", "gz", None)),
        check_vma=False,
    )
```

profile of v0, /device:TPU:14, one launch (start us, length us, event | category | flops | bytes accessed | tf_op | source)
XLA Modules:
  0.0 346.7 jit_solution(3024753138820903358)
XLA Ops:
  4.1 9.7 %collective-permute-start.1 = (f32[1,2,2,4,128]{4,2,1,3,0:T(2,128)S(1)}, f32[1,2,2,4,128]{4,2,1,3,0:T(2,128)S(1)}, u32[]{:S(2)}, u32[]{:S(2)}) collective-permute-start(f32[1,2,2,4,128]{4,2,1,3,0:T(2,128)S(1)} %get-tuple-element.743), channel_id=1, source_target_pairs={{32,0},{64,32},{96,64},{128,96},{160,128},{192,160},{224,192},{256... | collective-permute-start | bytes 24584 | tf_op jit(solution)/shard_map/ppermute | solution.py:16
  15.1 5.1 %collective-permute-start.2 = (f32[4,1,2,4,128]{4,2,1,3,0:T(2,128)S(1)}, f32[4,1,2,4,128]{4,2,1,3,0:T(2,128)S(1)}, u32[]{:S(2)}, u32[]{:S(2)}) collective-permute-start(f32[4,1,2,4,128]{4,2,1,3,0:T(2,128)S(1)} %get-tuple-element.736), channel_id=1, source_target_pairs={{0,8},{8,16},{16,24},{24,0},{1,9},{9,17},{17,25},{25,1},{2,10},{10... | collective-permute-start | bytes 49160 | tf_op jit(solution)/shard_map/ppermute | solution.py:13
  22.2 5.5 %collective-permute-done.3 = f32[4,1,2,4,128]{4,2,1,3,0:T(2,128)S(1)} collective-permute-done((f32[4,1,2,4,128]{4,2,1,3,0:T(2,128)S(1)}, f32[4,1,2,4,128]{4,2,1,3,0:T(2,128)S(1)}, u32[]{:S(2)}, u32[]{:S(2)}) %collective-permute-start.3) | collective-permute-done | bytes 16416 | tf_op jit(solution)/shard_map/ppermute | solution.py:16
  27.8 5.2 %collective-permute-start.4 = (f32[4,4,1,4,128]{4,2,1,3,0:T(1,128)S(1)}, f32[4,4,1,4,128]{4,2,1,3,0:T(1,128)S(1)}, u32[]{:S(2)}, u32[]{:S(2)}) collective-permute-start(f32[4,4,1,4,128]{4,2,1,3,0:T(1,128)S(1)} %get-tuple-element.730), channel_id=1, source_target_pairs={{0,1},{1,2},{2,3},{3,4},{4,5},{5,6},{6,7},{7,0},{8,9},{9,10},{10,1... | collective-permute-start | bytes 98312 | tf_op jit(solution)/shard_map/ppermute | solution.py:13
  33.0 14.0 %collective-permute-start.5 = (f32[4,4,1,4,128]{4,2,1,3,0:T(1,128)S(1)}, f32[4,4,1,4,128]{4,2,1,3,0:T(1,128)S(1)}, u32[]{:S(2)}, u32[]{:S(2)}) collective-permute-start(f32[4,4,1,4,128]{4,2,1,3,0:T(1,128)S(1)} %get-tuple-element.731), channel_id=1, source_target_pairs={{1,0},{2,1},{3,2},{4,3},{5,4},{6,5},{7,6},{0,7},{9,8},{10,9},{11,1... | collective-permute-start | bytes 98312 | tf_op jit(solution)/shard_map/ppermute | solution.py:16
  48.7 45.3 %while.106 = (s32[]{:T(128)}, f32[2,2,2,1,128]{4,2,1,3,0:T(2,128)S(1)}, s32[2]{0:T(128)S(1)}, f32[4,4,4,4,128]{4,2,1,3,0:T(4,128)S(1)}, s32[]{:T(128)}, /*index=...) while((s32[]{:T(128)}, ...), condition=%wide.region_5.6_spmd, body=%wide.region_0.5_spmd.sunk | while | flops 1376823 | bytes 826146 | solution.py:105
  51.0 20.3 %while.111 = (s32[]{:T(128)}, f32[2,2,1,128]{3,1,0,2:T(2,128)S(1)}, f32[2,2,4,128]{3,2,1,0:T(4,128)S(1)}, f32[3,4,4,4,128]{4,2,1,3,0:T(4,128)S(1)}, s32[]{:T(128...) while((s32[]{:T(128)}, f32[2,2,1,128]{3,1,0,2:T(2,128)S(1)}, ...), condition=%wide.region_4.4_spmd.clone, body=%wide.region_1.3_spmd.clone.sunk | while | flops 1376816 | bytes 592367 | solution.py:103
  73.6 20.3 %while.111 = (s32[]{:T(128)}, f32[2,2,1,128]{3,1,0,2:T(2,128)S(1)}, f32[2,2,4,128]{3,2,1,0:T(4,128)S(1)}, f32[3,4,4,4,128]{4,2,1,3,0:T(4,128)S(1)}, s32[]{:T(128...) while((s32[]{:T(128)}, f32[2,2,1,128]{3,1,0,2:T(2,128)S(1)}, ...), condition=%wide.region_4.4_spmd.clone, body=%wide.region_1.3_spmd.clone.sunk | while | flops 1376816 | bytes 592367 | solution.py:103
  94.7 1.9 collective-permute-start.6
  96.7 9.7 %collective-permute-start.7 = (f32[1,2,2,5,128]{4,2,1,3,0:T(2,128)S(1)}, f32[1,2,2,5,128]{4,2,1,3,0:T(2,128)S(1)}, u32[]{:S(2)}, u32[]{:S(2)}) collective-permute-start(f32[1,2,2,5,128]{4,2,1,3,0:T(2,128)S(1)} %get-tuple-element.741), channel_id=1, source_target_pairs={{32,0},{64,32},{96,64},{128,96},{160,128},{192,160},{224,192},{256... | collective-permute-start | bytes 30728 | tf_op jit(solution)/shard_map/ppermute | solution.py:16
  107.7 1.9 collective-permute-start.8
  109.7 3.9 %collective-permute-start.9 = (f32[4,1,2,5,128]{4,2,1,3,0:T(2,128)S(1)}, f32[4,1,2,5,128]{4,2,1,3,0:T(2,128)S(1)}, u32[]{:S(2)}, u32[]{:S(2)}) collective-permute-start(f32[4,1,2,5,128]{4,2,1,3,0:T(2,128)S(1)} %get-tuple-element.735), channel_id=1, source_target_pairs={{8,0},{16,8},{24,16},{0,24},{9,1},{17,9},{25,17},{1,25},{10,2},{18... | collective-permute-start | bytes 61448 | tf_op jit(solution)/shard_map/ppermute | solution.py:16
  113.6 3.5 %collective-permute-done.9 = f32[4,1,2,5,128]{4,2,1,3,0:T(2,128)S(1)} collective-permute-done((f32[4,1,2,5,128]{4,2,1,3,0:T(2,128)S(1)}, f32[4,1,2,5,128]{4,2,1,3,0:T(2,128)S(1)}, u32[]{:S(2)}, u32[]{:S(2)}) %collective-permute-start.9) | collective-permute-done | bytes 20512 | tf_op jit(solution)/shard_map/ppermute | solution.py:16
  119.2 5.4 %collective-permute-start.11 = (f32[4,4,1,5,128]{4,2,1,3,0:T(1,128)S(1)}, f32[4,4,1,5,128]{4,2,1,3,0:T(1,128)S(1)}, u32[]{:S(2)}, u32[]{:S(2)}) collective-permute-start(f32[4,4,1,5,128]{4,2,1,3,0:T(1,128)S(1)} %get-tuple-element.729), channel_id=1, source_target_pairs={{1,0},{2,1},{3,2},{4,3},{5,4},{6,5},{7,6},{0,7},{9,8},{10,9},{11,1... | collective-permute-start | bytes 122888 | tf_op jit(solution)/shard_map/ppermute | solution.py:16
  126.5 70.4 %while.108 = (s32[]{:T(128)}, f32[2,2,2,3,128]{4,2,1,3,0:T(2,128)S(1)}, s32[2]{0:T(128)S(1)}, f32[4,4,4,9,128]{4,2,1,3,0:T(4,128)S(1)}, s32[2,2,2,27]{3,2,1,0:T(...) while((s32[]{:T(128)}, ...), condition=%wide.region_14.15_spmd, body=%wide.region_6.14_spmd.sunk | while | flops 2236069 | bytes 1759827 | solution.py:105
  130.0 31.7 %while.112 = (s32[]{:T(128)}, f32[2,2,3,128]{3,1,0,2:T(2,128)S(1)}, f32[3,4,4,9,128]{4,2,1,3,0:T(4,128)S(1)}, f32[2,2,9,128]{3,2,1,0:T(8,128)S(1)}, f32[2,2,27]{...) while((s32[]{:T(128)}, f32[2,2,3,128]{3,1,0,2:T(2,128)S(1)}, ...), condition=%wide.region_13.13_spmd.clone, body=%wide.region_7.12_spmd.clone.sunk | while | flops 2235952 | bytes 1229355 | solution.py:103
  165.2 31.7 %while.112 = (s32[]{:T(128)}, f32[2,2,3,128]{3,1,0,2:T(2,128)S(1)}, f32[3,4,4,9,128]{4,2,1,3,0:T(4,128)S(1)}, f32[2,2,9,128]{3,2,1,0:T(8,128)S(1)}, f32[2,2,27]{...) while((s32[]{:T(128)}, f32[2,2,3,128]{3,1,0,2:T(2,128)S(1)}, ...), condition=%wide.region_13.13_spmd.clone, body=%wide.region_7.12_spmd.clone.sunk | while | flops 2235952 | bytes 1229355 | solution.py:103
  199.6 9.7 %collective-permute-start.13 = (f32[1,2,2,3,128]{4,2,1,3,0:T(2,128)S(1)}, f32[1,2,2,3,128]{4,2,1,3,0:T(2,128)S(1)}, u32[]{:S(2)}, u32[]{:S(2)}) collective-permute-start(f32[1,2,2,3,128]{4,2,1,3,0:T(2,128)S(1)} %get-tuple-element.745), channel_id=1, source_target_pairs={{32,0},{64,32},{96,64},{128,96},{160,128},{192,160},{224,192},{256... | collective-permute-start | bytes 18440 | tf_op jit(solution)/shard_map/ppermute | solution.py:16
  212.6 3.9 %collective-permute-start.15 = (f32[4,1,2,3,128]{4,2,1,3,0:T(2,128)S(1)}, f32[4,1,2,3,128]{4,2,1,3,0:T(2,128)S(1)}, u32[]{:S(2)}, u32[]{:S(2)}) collective-permute-start(f32[4,1,2,3,128]{4,2,1,3,0:T(2,128)S(1)} %get-tuple-element.739), channel_id=1, source_target_pairs={{8,0},{16,8},{24,16},{0,24},{9,1},{17,9},{25,17},{1,25},{10,2},{18... | collective-permute-start | bytes 36872 | tf_op jit(solution)/shard_map/ppermute | solution.py:16
  216.5 3.4 collective-permute-done.15
  222.0 5.4 %collective-permute-start.17 = (f32[4,4,1,3,128]{4,2,1,3,0:T(1,128)S(1)}, f32[4,4,1,3,128]{4,2,1,3,0:T(1,128)S(1)}, u32[]{:S(2)}, u32[]{:S(2)}) collective-permute-start(f32[4,4,1,3,128]{4,2,1,3,0:T(1,128)S(1)} %get-tuple-element.733), channel_id=1, source_target_pairs={{1,0},{2,1},{3,2},{4,3},{5,4},{6,5},{7,6},{0,7},{9,8},{10,9},{11,1... | collective-permute-start | bytes 73736 | tf_op jit(solution)/shard_map/ppermute | solution.py:16
  229.2 116.2 %while.110 = (s32[]{:T(128)}, f32[2,2,2,4,128]{4,3,2,1,0:T(4,128)S(1)}, s32[2]{0:T(128)S(1)}, f32[4,4,4,12,128]{4,2,1,3,0:T(4,128)S(1)}, s32[2,2,2,27]{3,2,1,0:T...) while((s32[]{:T(128)}, ...), condition=%wide.region_22.23_spmd, body=%wide.region_15.22_spmd.sunk | while | flops 3748517 | bytes 2785919 | solution.py:105
  232.7 54.6 %while.113 = (s32[]{:T(128)}, f32[2,2,4,128]{3,2,1,0:T(4,128)S(1)}, f32[2,2,12,128]{3,1,0,2:T(2,128)S(1)}, f32[3,4,4,12,128]{4,2,1,3,0:T(4,128)S(1)}, f32[2,2,12...) while((s32[]{:T(128)}, f32[2,2,4,128]{3,2,1,0:T(4,128)S(1)}, ...), condition=%wide.region_21.21_spmd.clone, body=%wide.region_16.20_spmd.clone.sunk | while | flops 3746864 | bytes 2118215 | solution.py:103
  290.8 54.6 %while.113 = (s32[]{:T(128)}, f32[2,2,4,128]{3,2,1,0:T(4,128)S(1)}, f32[2,2,12,128]{3,1,0,2:T(2,128)S(1)}, f32[3,4,4,12,128]{4,2,1,3,0:T(4,128)S(1)}, f32[2,2,12...) while((s32[]{:T(128)}, f32[2,2,4,128]{3,2,1,0:T(4,128)S(1)}, ...), condition=%wide.region_21.21_spmd.clone, body=%wide.region_16.20_spmd.clone.sunk | while | flops 3746864 | bytes 2118215 | solution.py:103
  (2110 shorter events, 222.5 us)
Async XLA Ops:
  1.4 13.7 %copy-start = (f32[2,2,2,3,128]{4,2,3,1,0:T(2,128)S(1)}, f32[2,2,2,3,128]{4,2,3,1,0:T(2,128)}, u32[]{:S(2)}) copy-start(f32[2,2,2,3,128]{4,2,3,1,0:T(2,128)} %param.18) | copy-start | bytes 36868
  2.2 11.6 %collective-permute-start = (f32[1,2,2,4,128]{4,2,1,3,0:T(2,128)S(1)}, f32[1,2,2,4,128]{4,2,1,3,0:T(2,128)S(1)}, u32[]{:S(2)}, u32[]{:S(2)}) collective-permute-start(f32[1,2,2,4,128]{4,2,1,3,0:T(2,128)S(1)} %get-tuple-element.742), channel_id=1, source_target_pairs={{0,32},{32,64},{64,96},{96,128},{128,160},{160,192},{192,224},{224... | collective-permute-start | bytes 24584 | tf_op jit(solution)/shard_map/ppermute | solution.py:13
  4.1 11.0 %collective-permute-start.1 = (f32[1,2,2,4,128]{4,2,1,3,0:T(2,128)S(1)}, f32[1,2,2,4,128]{4,2,1,3,0:T(2,128)S(1)}, u32[]{:S(2)}, u32[]{:S(2)}) collective-permute-start(f32[1,2,2,4,128]{4,2,1,3,0:T(2,128)S(1)} %get-tuple-element.743), channel_id=1, source_target_pairs={{32,0},{64,32},{96,64},{128,96},{160,128},{192,160},{224,192},{256... | collective-permute-start | bytes 24584 | tf_op jit(solution)/shard_map/ppermute | solution.py:16
  15.1 7.0 %collective-permute-start.2 = (f32[4,1,2,4,128]{4,2,1,3,0:T(2,128)S(1)}, f32[4,1,2,4,128]{4,2,1,3,0:T(2,128)S(1)}, u32[]{:S(2)}, u32[]{:S(2)}) collective-permute-start(f32[4,1,2,4,128]{4,2,1,3,0:T(2,128)S(1)} %get-tuple-element.736), channel_id=1, source_target_pairs={{0,8},{8,16},{16,24},{24,0},{1,9},{9,17},{17,25},{25,1},{2,10},{10... | collective-permute-start | bytes 49160 | tf_op jit(solution)/shard_map/ppermute | solution.py:13
  20.2 7.4 %collective-permute-start.3 = (f32[4,1,2,4,128]{4,2,1,3,0:T(2,128)S(1)}, f32[4,1,2,4,128]{4,2,1,3,0:T(2,128)S(1)}, u32[]{:S(2)}, u32[]{:S(2)}) collective-permute-start(f32[4,1,2,4,128]{4,2,1,3,0:T(2,128)S(1)} %get-tuple-element.737), channel_id=1, source_target_pairs={{8,0},{16,8},{24,16},{0,24},{9,1},{17,9},{25,17},{1,25},{10,2},{18... | collective-permute-start | bytes 49160 | tf_op jit(solution)/shard_map/ppermute | solution.py:16
  27.8 19.3 %collective-permute-start.4 = (f32[4,4,1,4,128]{4,2,1,3,0:T(1,128)S(1)}, f32[4,4,1,4,128]{4,2,1,3,0:T(1,128)S(1)}, u32[]{:S(2)}, u32[]{:S(2)}) collective-permute-start(f32[4,4,1,4,128]{4,2,1,3,0:T(1,128)S(1)} %get-tuple-element.730), channel_id=1, source_target_pairs={{0,1},{1,2},{2,3},{3,4},{4,5},{5,6},{6,7},{7,0},{8,9},{9,10},{10,1... | collective-permute-start | bytes 98312 | tf_op jit(solution)/shard_map/ppermute | solution.py:13
  33.0 15.6 %collective-permute-start.5 = (f32[4,4,1,4,128]{4,2,1,3,0:T(1,128)S(1)}, f32[4,4,1,4,128]{4,2,1,3,0:T(1,128)S(1)}, u32[]{:S(2)}, u32[]{:S(2)}) collective-permute-start(f32[4,4,1,4,128]{4,2,1,3,0:T(1,128)S(1)} %get-tuple-element.731), channel_id=1, source_target_pairs={{1,0},{2,1},{3,2},{4,3},{5,4},{6,5},{7,6},{0,7},{9,8},{10,9},{11,1... | collective-permute-start | bytes 98312 | tf_op jit(solution)/shard_map/ppermute | solution.py:16
  48.7 45.4 %copy-start.1 = (f32[2,2,2,3,128]{4,2,3,1,0:T(2,128)S(1)}, f32[2,2,2,3,128]{4,2,3,1,0:T(2,128)}, u32[]{:S(2)}) copy-start(f32[2,2,2,3,128]{4,2,3,1,0:T(2,128)} %param.19) | copy-start | bytes 36868
  94.0 0.7 copy-start.2
  94.7 11.6 %collective-permute-start.6 = (f32[1,2,2,5,128]{4,2,1,3,0:T(2,128)S(1)}, f32[1,2,2,5,128]{4,2,1,3,0:T(2,128)S(1)}, u32[]{:S(2)}, u32[]{:S(2)}) collective-permute-start(f32[1,2,2,5,128]{4,2,1,3,0:T(2,128)S(1)} %get-tuple-element.740), channel_id=1, source_target_pairs={{0,32},{32,64},{64,96},{96,128},{128,160},{160,192},{192,224},{224... | collective-permute-start | bytes 30728 | tf_op jit(solution)/shard_map/ppermute | solution.py:13
  96.7 11.0 %collective-permute-start.7 = (f32[1,2,2,5,128]{4,2,1,3,0:T(2,128)S(1)}, f32[1,2,2,5,128]{4,2,1,3,0:T(2,128)S(1)}, u32[]{:S(2)}, u32[]{:S(2)}) collective-permute-start(f32[1,2,2,5,128]{4,2,1,3,0:T(2,128)S(1)} %get-tuple-element.741), channel_id=1, source_target_pairs={{32,0},{64,32},{96,64},{128,96},{160,128},{192,160},{224,192},{256... | collective-permute-start | bytes 30728 | tf_op jit(solution)/shard_map/ppermute | solution.py:16
  107.7 5.9 %collective-permute-start.8 = (f32[4,1,2,5,128]{4,2,1,3,0:T(2,128)S(1)}, f32[4,1,2,5,128]{4,2,1,3,0:T(2,128)S(1)}, u32[]{:S(2)}, u32[]{:S(2)}) collective-permute-start(f32[4,1,2,5,128]{4,2,1,3,0:T(2,128)S(1)} %get-tuple-element.734), channel_id=1, source_target_pairs={{0,8},{8,16},{16,24},{24,0},{1,9},{9,17},{17,25},{25,1},{2,10},{10... | collective-permute-start | bytes 61448 | tf_op jit(solution)/shard_map/ppermute | solution.py:13
  109.7 7.5 %collective-permute-start.9 = (f32[4,1,2,5,128]{4,2,1,3,0:T(2,128)S(1)}, f32[4,1,2,5,128]{4,2,1,3,0:T(2,128)S(1)}, u32[]{:S(2)}, u32[]{:S(2)}) collective-permute-start(f32[4,1,2,5,128]{4,2,1,3,0:T(2,128)S(1)} %get-tuple-element.735), channel_id=1, source_target_pairs={{8,0},{16,8},{24,16},{0,24},{9,1},{17,9},{25,17},{1,25},{10,2},{18... | collective-permute-start | bytes 61448 | tf_op jit(solution)/shard_map/ppermute | solution.py:16
  117.3 7.4 %collective-permute-start.10 = (f32[4,4,1,5,128]{4,2,1,3,0:T(1,128)S(1)}, f32[4,4,1,5,128]{4,2,1,3,0:T(1,128)S(1)}, u32[]{:S(2)}, u32[]{:S(2)}) collective-permute-start(f32[4,4,1,5,128]{4,2,1,3,0:T(1,128)S(1)} %get-tuple-element.728), channel_id=1, source_target_pairs={{0,1},{1,2},{2,3},{3,4},{4,5},{5,6},{6,7},{7,0},{8,9},{9,10},{10,1... | collective-permute-start | bytes 122888 | tf_op jit(solution)/shard_map/ppermute | solution.py:13
  119.2 7.1 %collective-permute-start.11 = (f32[4,4,1,5,128]{4,2,1,3,0:T(1,128)S(1)}, f32[4,4,1,5,128]{4,2,1,3,0:T(1,128)S(1)}, u32[]{:S(2)}, u32[]{:S(2)}) collective-permute-start(f32[4,4,1,5,128]{4,2,1,3,0:T(1,128)S(1)} %get-tuple-element.729), channel_id=1, source_target_pairs={{1,0},{2,1},{3,2},{4,3},{5,4},{6,5},{7,6},{0,7},{9,8},{10,9},{11,1... | collective-permute-start | bytes 122888 | tf_op jit(solution)/shard_map/ppermute | solution.py:16
  124.6 1.9 copy-start.3
  197.0 0.7 copy-start.5
  197.7 11.6 %collective-permute-start.12 = (f32[1,2,2,3,128]{4,2,1,3,0:T(2,128)S(1)}, f32[1,2,2,3,128]{4,2,1,3,0:T(2,128)S(1)}, u32[]{:S(2)}, u32[]{:S(2)}) collective-permute-start(f32[1,2,2,3,128]{4,2,1,3,0:T(2,128)S(1)} %get-tuple-element.744), channel_id=1, source_target_pairs={{0,32},{32,64},{64,96},{96,128},{128,160},{160,192},{192,224},{224... | collective-permute-start | bytes 18440 | tf_op jit(solution)/shard_map/ppermute | solution.py:13
  199.6 11.0 %collective-permute-start.13 = (f32[1,2,2,3,128]{4,2,1,3,0:T(2,128)S(1)}, f32[1,2,2,3,128]{4,2,1,3,0:T(2,128)S(1)}, u32[]{:S(2)}, u32[]{:S(2)}) collective-permute-start(f32[1,2,2,3,128]{4,2,1,3,0:T(2,128)S(1)} %get-tuple-element.745), channel_id=1, source_target_pairs={{32,0},{64,32},{96,64},{128,96},{160,128},{192,160},{224,192},{256... | collective-permute-start | bytes 18440 | tf_op jit(solution)/shard_map/ppermute | solution.py:16
  210.7 5.9 %collective-permute-start.14 = (f32[4,1,2,3,128]{4,2,1,3,0:T(2,128)S(1)}, f32[4,1,2,3,128]{4,2,1,3,0:T(2,128)S(1)}, u32[]{:S(2)}, u32[]{:S(2)}) collective-permute-start(f32[4,1,2,3,128]{4,2,1,3,0:T(2,128)S(1)} %get-tuple-element.738), channel_id=1, source_target_pairs={{0,8},{8,16},{16,24},{24,0},{1,9},{9,17},{17,25},{25,1},{2,10},{10... | collective-permute-start | bytes 36872 | tf_op jit(solution)/shard_map/ppermute | solution.py:13
  212.6 7.4 %collective-permute-start.15 = (f32[4,1,2,3,128]{4,2,1,3,0:T(2,128)S(1)}, f32[4,1,2,3,128]{4,2,1,3,0:T(2,128)S(1)}, u32[]{:S(2)}, u32[]{:S(2)}) collective-permute-start(f32[4,1,2,3,128]{4,2,1,3,0:T(2,128)S(1)} %get-tuple-element.739), channel_id=1, source_target_pairs={{8,0},{16,8},{24,16},{0,24},{9,1},{17,9},{25,17},{1,25},{10,2},{18... | collective-permute-start | bytes 36872 | tf_op jit(solution)/shard_map/ppermute | solution.py:16
  220.0 7.4 %copy-start.4 = (s32[2,2,2]{2,1,0:T(2,128)S(1)}, s32[2,2,2]{2,1,0:T(2,128)}, u32[]{:S(2)}) copy-start(s32[2,2,2]{2,1,0:T(2,128)} %param.23) | copy-start | bytes 100
  220.1 7.5 %collective-permute-start.16 = (f32[4,4,1,3,128]{4,2,1,3,0:T(1,128)S(1)}, f32[4,4,1,3,128]{4,2,1,3,0:T(1,128)S(1)}, u32[]{:S(2)}, u32[]{:S(2)}) collective-permute-start(f32[4,4,1,3,128]{4,2,1,3,0:T(1,128)S(1)} %get-tuple-element.732), channel_id=1, source_target_pairs={{0,1},{1,2},{2,3},{3,4},{4,5},{5,6},{6,7},{7,0},{8,9},{9,10},{10,1... | collective-permute-start | bytes 73736 | tf_op jit(solution)/shard_map/ppermute | solution.py:13
  222.0 7.0 %collective-permute-start.17 = (f32[4,4,1,3,128]{4,2,1,3,0:T(1,128)S(1)}, f32[4,4,1,3,128]{4,2,1,3,0:T(1,128)S(1)}, u32[]{:S(2)}, u32[]{:S(2)}) collective-permute-start(f32[4,4,1,3,128]{4,2,1,3,0:T(1,128)S(1)} %get-tuple-element.733), channel_id=1, source_target_pairs={{1,0},{2,1},{3,2},{4,3},{5,4},{6,5},{7,6},{0,7},{9,8},{10,9},{11,1... | collective-permute-start | bytes 73736 | tf_op jit(solution)/shard_map/ppermute | solution.py:16
where the time goes:
time: 348 us; the launch traced here: 347 us
  other arithmetic  190 us (55%)
  starting transfers between devices  87.4 us (25%)
  loops' own time  34.8 us (10%)
  waiting for transfers between devices  21.1 us (6%)
  local copies, waits for them, and re-layouts  12.2 us (4%)
    ppermute x9, starting transfers between devices, extended(): lax.ppermute(lax.slice_in_dim(block, 0, width, axis=dim), axis, backward)  63.7 us
    reduce_sum x162, other arithmetic, pair_geometry(): radius = jnp.sqrt(jnp.sum(separation * separation, axis=2))  55.9 us
    reduce_sum x54, other arithmetic, force_terms(): accel = -jnp.sum(push[:, :, None] * separation, axis=-1)  38.9 us
    ppermute x9, starting transfers between devices, extended(): lax.ppermute(lax.slice_in_dim(block, block.shape[dim] - width, None, axis...  23.7 us
    ppermute x9, waiting for transfers between devices, extended(): lax.ppermute(lax.slice_in_dim(block, 0, width, axis=dim), axis, backward)  21.1 us
    reduce_sum x54, other arithmetic, force_terms(): jnp.sum(scaled * (specific_own + 0.5 * damping) * closing, axis=-1)  20.8 us
    another operation x6, loops' own time, leaf_row(): return lax.fori_loop(jnp.int32(0), jnp.int32(27), partner_step, start)  20.3 us
    reduce_sum x54, other arithmetic, density_terms(): summed_mass = jnp.sum(weight * mass_far * kernel, axis=-1)  20 us
  transfers between devices with their start and end apart: 18, of which 9 were waited for; matrix products, arithmetic and copies ran while one was open for 0% of the time, Pallas kernels for 0%

commit v1 on v0

v1 whole, which is shorter than its diff:
```python
import jax
import jax.numpy as jnp
from jax import lax
from jax.experimental import pallas as pl
from jax.experimental.pallas import tpu as pltpu
from jax.sharding import PartitionSpec as P

F32 = jnp.float32
MESH = pl.DeviceIdType.MESH
AXES = ("gx", "gy", "gz")
CHUNK = 32
FAR = 1.0e3
DIRECTIONS = [
    (dx, dy, dz)
    for dx in (-1, 0, 1)
    for dy in (-1, 0, 1)
    for dz in (-1, 0, 1)
    if (dx, dy, dz) != (0, 0, 0)
]
LEAVES = [(ix, iy, iz) for ix in range(2) for iy in range(2) for iz in range(2)]
DIGITS = [(a, b, c) for a in range(3) for b in range(3) for c in range(3)]
INSIDE = [d for d in DIGITS if max(d) < 2]
OUTSIDE = [d for d in DIGITS if max(d) == 2]


def own_span(step):
    return {1: pl.ds(2, 1), -1: pl.ds(1, 1), 0: pl.ds(1, 2)}[step]


def halo_span(step):
    return {1: pl.ds(0, 1), -1: pl.ds(3, 1), 0: pl.ds(1, 2)}[step]


def neighbours():
    found = []
    for direction in DIRECTIONS:
        found.append(
            tuple(
                lax.rem(lax.axis_index(axis) + (step + lax.axis_size(axis)), lax.axis_size(axis))
                for axis, step in zip(AXES, direction)
            )
        )
    return found


def exchange(field, devices, send_sems, recv_sems):
    copies = []
    for index, direction in enumerate(DIRECTIONS):
        source = tuple(own_span(step) for step in direction)
        target = tuple(halo_span(step) for step in direction)
        copies.append(
            pltpu.make_async_remote_copy(
                src_ref=field.at[source],
                dst_ref=field.at[target],
                send_sem=send_sems.at[index],
                recv_sem=recv_sems.at[index],
                device_id=devices[index],
                device_id_type=MESH,
            )
        )
    for copy in copies:
        copy.start()
    return copies


def partner_of(leaf, digits):
    place = tuple(1 + d if d < 2 else 3 * i for i, d in zip(leaf, digits))
    offset = tuple(j - 1 - i for j, i in zip(place, leaf))
    number = 9 * (offset[0] + 1) + 3 * (offset[1] + 1) + offset[2] + 1
    return place, offset, number


def leaf_at(index):
    return (index // 4, (index // 2) % 2, index % 2)


def kernel(
    offsets_ref,
    velocity_ref,
    mass_ref,
    energy_ref,
    mask_ref,
    counts_ref,
    accel_ref,
    rate_ref,
    base,
    ratio,
    state,
    own,
    columns,
    far_columns,
    sums,
    mass_w,
    mass_g,
    mass_e,
    table,
    send_sems,
    recv_sems,
):
    devices = neighbours()
    barrier = pltpu.get_barrier_semaphore()
    for device in devices:
        pl.semaphore_signal(barrier, inc=1, device_id=device, device_id_type=MESH)

    slot = lax.broadcasted_iota(jnp.int32, (1, 128), 1)
    own[...] = jnp.zeros_like(own)
    for number, (ix, iy, iz) in enumerate(LEAVES):
        valid = slot < counts_ref[ix, iy, iz]
        place = (1 + ix, 1 + iy, 1 + iz)
        for d in range(3):
            spot = jnp.where(valid, 2.0 * offsets_ref[ix, iy, iz, d : d + 1, :], FAR)
            speed = velocity_ref[ix, iy, iz, d : d + 1, :]
            base[place + (slice(d, d + 1),)] = spot
            base[place + (slice(4 + d, 5 + d),)] = speed
            own[8 * d + number : 8 * d + number + 1, :] = spot
            own[8 * (3 + d) + number : 8 * (3 + d) + number + 1, :] = speed
        weight = mass_ref[ix, iy, iz : iz + 1, :]
        base[place + (slice(3, 4),)] = weight
        base[place + (slice(7, 8),)] = weight
        own[48 + number : 49 + number, :] = weight
        own[56 + number : 57 + number, :] = energy_ref[ix, iy, iz : iz + 1, :]
        own[64 + number : 65 + number, :] = valid.astype(F32)

    copies = []
    pl.semaphore_wait(barrier, len(DIRECTIONS))
    first = exchange(base, devices, send_sems.at[0], recv_sems.at[0])
    copies += first

    turned = jnp.transpose(own[...])
    for f in range(6):
        for number in range(8):
            column = 8 * f + number
            columns[f, number] = jnp.broadcast_to(turned[:, column : column + 1], (128, 128))

    def over_chunks(body):
        def step(n, carry):
            body(n // (128 // CHUNK), (n % (128 // CHUNK)) * CHUNK)
            return carry

        lax.fori_loop(0, 8 * (128 // CHUNK), step, 0)

    def first_pass(digit_list, fresh):
        def body(number, start):
            leaf = leaf_at(number)
            rows = pl.ds(pl.multiple_of(start, CHUNK), CHUNK)
            if fresh:
                volume = jnp.zeros((CHUNK, 128), F32)
                weighed = jnp.zeros((CHUNK, 128), F32)
            else:
                volume = sums[0, number, rows, :]
                weighed = sums[1, number, rows, :]
            for digits in digit_list:
                place, offset, k = partner_of(leaf, digits)
                picked = mask_ref[leaf + (k,)].astype(F32)
                square = None
                closing = None
                for d in range(3):
                    far = base[place + (slice(d, d + 1),)] + 2.0 * offset[d].astype(F32)
                    gap = columns[d, number, rows, :] - far
                    rush = base[place + (slice(4 + d, 5 + d),)] - columns[3 + d, number, rows, :]
                    square = gap * gap if square is None else square + gap * gap
                    closing = rush * gap if closing is None else closing + rush * gap
                square = jnp.maximum(square, 1.0e-30)
                inside = jnp.maximum(2.0 - square * lax.rsqrt(square), 0.0)
                two = inside * inside
                weight = base[place + (slice(3, 4),)] * picked
                smooth = two * two * (2.5 - inside)
                volume = volume + smooth
                smooth = smooth * weight
                weighed = weighed + smooth
                slope = two * inside * weight
                mass_w[number, k, rows, :] = smooth
                mass_g[number, k, rows, :] = slope
                mass_e[number, k, rows, :] = slope * closing
            sums[0, number, rows, :] = volume
            sums[1, number, rows, :] = weighed

        over_chunks(body)

    def second_pass(digit_list, fresh):
        def body(number, start):
            leaf = leaf_at(number)
            rows = pl.ds(pl.multiple_of(start, CHUNK), CHUNK)
            if fresh:
                volume = jnp.zeros((CHUNK, 128), F32)
                spread = jnp.zeros((CHUNK, 128), F32)
            else:
                volume = sums[2, number, rows, :]
                spread = sums[3, number, rows, :]
            for digits in digit_list:
                place, offset, k = partner_of(leaf, digits)
                weight = ratio[place + (slice(0, 1),)]
                volume = volume + weight * mass_w[number, k, rows, :]
                spread = spread + weight * mass_e[number, k, rows, :]
            sums[2, number, rows, :] = volume
            sums[3, number, rows, :] = spread

        over_chunks(body)

    def third_pass(digit_list, fresh):
        def body(number, start):
            leaf = leaf_at(number)
            rows = pl.ds(pl.multiple_of(start, CHUNK), CHUNK)
            if fresh:
                totals = [jnp.zeros((CHUNK, 128), F32)] * 5
            else:
                totals = [sums[f, number, rows, :] for f in range(5)]
            for digits in digit_list:
                place, offset, k = partner_of(leaf, digits)
                dense = far_columns[0, number, rows, :] + state[place + (slice(0, 1),)]
                sticky = far_columns[1, number, rows, :] + state[place + (slice(1, 2),)]
                damp = sticky * pltpu.reciprocal(dense, approx=True)
                mine = far_columns[2, number, rows, :] + damp
                theirs = state[place + (slice(2, 3),)] + damp
                push = mass_g[number, k, rows, :] * (mine + theirs)
                totals[0] = totals[0] + push
                for d in range(3):
                    far = base[place + (slice(d, d + 1),)] + 2.0 * offset[d].astype(F32)
                    totals[1 + d] = totals[1 + d] + push * far
                totals[4] = totals[4] + mass_e[number, k, rows, :] * mine
            for f in range(5):
                sums[f, number, rows, :] = totals[f]

        over_chunks(body)

    lane = lax.broadcasted_iota(jnp.int32, (128, 128), 1)

    def gathered(fields):
        packed = jnp.zeros((128, 128), F32)
        for f in fields:
            for number in range(8):
                total = jnp.sum(sums[f, number], axis=1, keepdims=True)
                packed = jnp.where(lane == 8 * f + number, total, packed)
        table[...] = jnp.transpose(packed)

    first_pass(INSIDE, True)
    for copy in first:
        copy.wait_recv()
    first_pass(OUTSIDE, False)

    gathered((0, 1))
    mass = own[48:56, :]
    volume = 1.0 / (1.0 + 0.125 * table[0:8, :])
    summed_mass = mass + 0.125 * table[8:16, :]
    rated = volume / mass
    for number, (ix, iy, iz) in enumerate(LEAVES):
        ratio[1 + ix, 1 + iy, 1 + iz] = rated[number : number + 1, :]
    second = exchange(ratio, devices, send_sems.at[1], recv_sems.at[1])
    copies += second
    second_pass(INSIDE, True)
    for copy in second:
        copy.wait_recv()
    second_pass(OUTSIDE, False)

    gathered((2, 3))
    density = summed_mass / (volume + 0.125 * table[16:24, :])
    sticky = jnp.maximum(1.25 * table[24:32, :], 0.0)
    specific = (2.0 / 3.0) * own[56:64, :] / density
    for number, (ix, iy, iz) in enumerate(LEAVES):
        place = (1 + ix, 1 + iy, 1 + iz)
        for f, rows in enumerate((density, sticky, specific)):
            state[place + (slice(f, f + 1),)] = rows[number : number + 1, :]
        state[place + (slice(3, 4),)] = jnp.zeros((1, 128), F32)
    third = exchange(state, devices, send_sems.at[2], recv_sems.at[2])
    copies += third
    own[0:8, :] = density
    own[8:16, :] = sticky
    own[16:24, :] = specific
    turned = jnp.transpose(own[...])
    for f in range(3):
        for number in range(8):
            column = 8 * f + number
            far_columns[f, number] = jnp.broadcast_to(turned[:, column : column + 1], (128, 128))
    third_pass(INSIDE, True)
    for copy in third:
        copy.wait_recv()
    third_pass(OUTSIDE, False)

    gathered((0, 1, 2, 3, 4))
    for number, (ix, iy, iz) in enumerate(LEAVES):
        valid = own[64 + number : 65 + number, :] > 0.5
        total = table[number : number + 1, :]
        for d in range(3):
            row = 8 * (1 + d) + number
            spot = base[1 + ix, 1 + iy, 1 + iz, d : d + 1, :]
            value = 1.25 * (spot * total - table[row : row + 1, :])
            accel_ref[ix, iy, iz, d : d + 1, :] = jnp.where(valid, value, 0.0)
        rate_ref[ix, iy, iz : iz + 1, :] = jnp.where(
            valid, 1.25 * table[32 + number : 33 + number, :], 0.0
        )
    for copy in copies:
        copy.wait_send()


def shards(offsets, velocity, mass, energy, partner_mask, counts):
    vmem = pl.BlockSpec(memory_space=pltpu.VMEM)
    smem = pl.BlockSpec(memory_space=pltpu.SMEM)
    return pl.pallas_call(
        kernel,
        out_shape=(
            jax.ShapeDtypeStruct(offsets.shape, F32),
            jax.ShapeDtypeStruct(mass.shape, F32),
        ),
        in_specs=[vmem] * 4 + [smem] * 2,
        out_specs=(vmem, vmem),
        scratch_shapes=[
            pltpu.VMEM((4, 4, 4, 8, 128), F32),
            pltpu.VMEM((4, 4, 4, 1, 128), F32),
            pltpu.VMEM((4, 4, 4, 4, 128), F32),
            pltpu.VMEM((128, 128), F32),
            pltpu.VMEM((6, 8, 128, 128), F32),
            pltpu.VMEM((3, 8, 128, 128), F32),
            pltpu.VMEM((5, 8, 128, 128), F32),
            pltpu.VMEM((8, 27, 128, 128), F32),
            pltpu.VMEM((8, 27, 128, 128), F32),
            pltpu.VMEM((8, 27, 128, 128), F32),
            pltpu.VMEM((128, 128), F32),
            pltpu.SemaphoreType.DMA((3, 26)),
            pltpu.SemaphoreType.DMA((3, 26)),
        ],
        compiler_params=pltpu.CompilerParams(
            collective_id=0,
            has_side_effects=True,
            vmem_limit_bytes=60 * 1024 * 1024,
        ),
    )(offsets, velocity, mass, energy, partner_mask, counts)


def solution(mesh):
    placed = (
        P("gx", "gy", "gz", None, None),
        P("gx", "gy", "gz", None, None),
        P("gx", "gy", "gz", None),
        P("gx", "gy", "gz", None),
        P("gx", "gy", "gz", None),
        P("gx", "gy", "gz"),
    )
    return jax.shard_map(
        shards,
        mesh=mesh,
        in_specs=placed,
        out_specs=(P("gx", "gy", "gz", None, None), P("gx", "gy", "gz", None)),
        check_vma=False,
    )
```

time: 348 us -> 76.4 us (0.22)
  the two profiles are of different devices: /device:TPU:14 before, /device:TPU:1 now
where the time goes in v1:
time: 76.4 us; the launch traced here: 75.4 us
  Pallas kernels  70.9 us (93%)
  local copies, waits for them, and re-layouts  3.85 us (5%)
    pallas_call x1, Pallas kernels, shards(): pl.pallas_call(kernel, out_shape=(jax.ShapeDtypeStruct(offsets.shape, F32...  70.9 us
    unnamed x7, local copies, waits for them, and re-layouts  2.52 us

profile of v1, /device:TPU:1, one launch (start us, length us, event | category | flops | bytes accessed | tf_op | source)
XLA Modules:
  0.0 75.4 jit_solution(8461611788622800435)
XLA Ops:
  0.6 0.0 copy-start
  0.6 1.3 %copy.8.offsets_ref = f32[2,2,2,3,128]{4,3,2,1,0:T(4,128)} copy(f32[2,2,2,3,128]{4,2,3,1,0:T(2,128)} %param.6) | data formatting | bytes 24576 | tf_op args[0]
  2.0 0.0 copy-done
  2.0 0.6 copy.9.velocity_ref
  2.6 70.9 %shard_map.77 = (f32[2,2,2,3,128]{4,3,2,1,0:T(4,128)}, f32[2,2,2,128]{3,2,1,0:T(2,128)}) custom-call(f32[2,2,2,3,128]{4,3,2,1,0:T(4,128)} %copy.8.offsets_ref, f32[2,2,2,3,128]{4,3,2,1,0:T(4,128)} %copy.9.velocity_ref, f32[2,2,2,128]{3,2,1,0:T(2,128)} %mass_ref.1, f32[2,2,2,128]{3,2,1,0:T(2,128)} %energy_ref.1, s32[2,2,2,27]{3,2,1,0:T(2,128)} %mask_ref.1, ...), custom_call_target="tpu_custom_call" | custom-call | tf_op jit(solution)/shard_map/pallas_call | solution.py:298
  73.4 0.0 copy-start.1
  73.5 1.3 %copy.10 = f32[2,2,2,3,128]{4,2,3,1,0:T(2,128)} copy(f32[2,2,2,3,128]{4,3,2,1,0:T(4,128)} %get-tuple-element.2) | data formatting | bytes 24576 | tf_op jit(solution)/shard_map/pallas_call | solution.py:298
  74.8 0.0 copy-done.1
  74.8 0.6 copy.12
Async XLA Ops:
  0.6 1.3 %copy-start = (f32[2,2,2,3,128]{4,2,3,1,0:T(2,128)S(1)}, f32[2,2,2,3,128]{4,2,3,1,0:T(2,128)}, u32[]{:S(2)}) copy-start(f32[2,2,2,3,128]{4,2,3,1,0:T(2,128)} %param.7) | copy-start | bytes 36868
  73.4 1.3 %copy-start.1 = (f32[2,2,2,128]{3,2,1,0:T(2,128)S(1)}, f32[2,2,2,128]{3,2,1,0:T(2,128)}, u32[]{:S(2)}) copy-start(f32[2,2,2,128]{3,2,1,0:T(2,128)} %get-tuple-element.7) | copy-start | bytes 12292

commit v2 on v1

v2 whole, which is shorter than its diff:
```python
import jax
import jax.numpy as jnp
from jax import lax
from jax.experimental import pallas as pl
from jax.experimental.pallas import tpu as pltpu
from jax.sharding import PartitionSpec as P

F32 = jnp.float32
BF16 = jnp.bfloat16
MESH = pl.DeviceIdType.MESH
AXES = ("gx", "gy", "gz")
FAR = 1.0e2
DEPTH = 80
DIRECTIONS = [
    (dx, dy, dz)
    for dz in (1, 0, -1)
    for dx in (-1, 0, 1)
    for dy in (-1, 0, 1)
    if (dx, dy, dz) != (0, 0, 0)
]
UPWARD = 9
EVERY = range(len(DIRECTIONS))
LEAVES = [(ix, iy, iz) for ix in range(2) for iy in range(2) for iz in range(2)]
DIGITS = [(a, b, c) for a in range(3) for b in range(3) for c in range(3)]
INSIDE = [d for d in DIGITS if max(d) < 2]
BESIDE = [d for d in DIGITS if max(d) == 2 and d[2] < 2]
BEYOND = [d for d in DIGITS if d[2] == 2]


def own_span(step):
    return {1: pl.ds(2, 1), -1: pl.ds(1, 1), 0: pl.ds(1, 2)}[step]


def halo_span(step):
    return {1: pl.ds(0, 1), -1: pl.ds(3, 1), 0: pl.ds(1, 2)}[step]


def neighbours():
    found = []
    for direction in DIRECTIONS:
        found.append(
            tuple(
                lax.rem(lax.axis_index(axis) + (step + lax.axis_size(axis)), lax.axis_size(axis))
                for axis, step in zip(AXES, direction)
            )
        )
    return found


def exchange(field, devices, send_sems, recv_sems, indices):
    copies = []
    for index in indices:
        direction = DIRECTIONS[index]
        copies.append(
            pltpu.make_async_remote_copy(
                src_ref=field.at[tuple(own_span(step) for step in direction)],
                dst_ref=field.at[tuple(halo_span(step) for step in direction)],
                send_sem=send_sems.at[index],
                recv_sem=recv_sems.at[index],
                device_id=devices[index],
                device_id_type=MESH,
            )
        )
    for copy in copies:
        copy.start()
    return copies


def partners(leaf, digit_list):
    places, steps = [], []
    for axis, i in enumerate(leaf):
        places.append((1, 2, 3 * i))
        steps.append([3 ** (2 - axis) * (j - i) for j in places[-1]])
    for digits in digit_list:
        yield (
            tuple(places[axis][d] for axis, d in enumerate(digits)),
            sum(steps[axis][d] for axis, d in enumerate(digits)),
            DIGITS.index(digits),
        )


def kernel(
    offsets_ref,
    velocity_ref,
    mass_ref,
    energy_ref,
    mask_ref,
    counts_ref,
    accel_ref,
    rate_ref,
    base,
    placed,
    ratio,
    state,
    own,
    near_terms,
    far_terms,
    far_columns,
    sums,
    mass_w,
    mass_g,
    mass_e,
    pack,
    table,
    send_sems,
    recv_sems,
):
    devices = neighbours()
    barrier = pltpu.get_barrier_semaphore()
    for device in devices:
        pl.semaphore_signal(barrier, inc=1, device_id=device, device_id_type=MESH)

    slot = lax.broadcasted_iota(jnp.int32, (1, 128), 1)
    own[...] = jnp.zeros_like(own)
    for number, (ix, iy, iz) in enumerate(LEAVES):
        valid = slot < counts_ref[ix, iy, iz]
        place = (1 + ix, 1 + iy, 1 + iz)
        for d in range(3):
            spot = jnp.where(valid, 2.0 * offsets_ref[ix, iy, d, iz : iz + 1, :], FAR)
            base[place + (slice(d, d + 1),)] = spot
            base[place + (slice(4 + d, 5 + d),)] = velocity_ref[ix, iy, d, iz : iz + 1, :]
        weight = mass_ref[ix, iy, iz : iz + 1, :]
        base[place + (slice(3, 4),)] = weight
        base[place + (slice(7, 8),)] = weight
        own[48 + number : 49 + number, :] = weight
        own[56 + number : 57 + number, :] = energy_ref[ix, iy, iz : iz + 1, :]
        own[64 + number : 65 + number, :] = valid.astype(F32)

    pl.semaphore_wait(barrier, len(DIRECTIONS))
    first = exchange(base, devices, send_sems.at[0], recv_sems.at[0], EVERY)

    line = lax.broadcasted_iota(jnp.int32, (8, 128), 0)

    def marked(*chosen):
        found = line == chosen[0]
        for row in chosen[1:]:
            found = found | (line == row)
        return found.astype(F32)

    axes = [marked(d) for d in range(3)]
    positions = marked(0, 1, 2)
    both = marked(0, 1, 2, 4, 5, 6)
    one, last = marked(3), marked(7)
    nothing = jnp.zeros((8, 128), F32)

    def framed(place):
        shift = sum(axes[d] * jnp.float32(2 * (place[d] - 2)) for d in range(3))
        return base[place] + shift

    def split(rows):
        high = rows.astype(BF16).astype(F32)
        rest = rows - high
        middle = rest.astype(BF16).astype(F32)
        return high, middle, rest - middle

    def make_far(place):
        rows = framed(place)
        placed[place] = rows
        swapped = pltpu.roll(rows, 4, 0)
        halves = []
        for linear, product in (
            (rows * (-2.0 * positions) + one, rows * rows),
            (swapped * both - last, -(rows * swapped)),
        ):
            high, middle, low = split(linear)
            parts = [high, high, high, middle, middle, low, *split(product), nothing]
            halves.append(jnp.concatenate(parts, axis=0))
        far_terms[place] = jnp.concatenate(halves, axis=1).astype(BF16)

    def make_near(number, place):
        rows = framed(place)
        swapped = pltpu.roll(rows, 4, 0)
        square = jnp.sum(rows * rows * positions, axis=0, keepdims=True)
        along = jnp.sum(rows * swapped * positions, axis=0, keepdims=True)
        rows = rows * both + one * square + last * along
        high, middle, low = split(rows)
        parts = [high, middle, low, high, middle, high, positions, positions, positions]
        parts += [nothing] * 7
        near_terms[number] = jnp.transpose(jnp.concatenate(parts, axis=0))[:, 0:DEPTH].astype(BF16)

    for number, (ix, iy, iz) in enumerate(LEAVES):
        make_near(number, (1 + ix, 1 + iy, 1 + iz))
        make_far((1 + ix, 1 + iy, 1 + iz))

    def make_outer_far(levels):
        for place in [(x, y, z) for x in range(4) for y in range(4) for z in levels]:
            if any(j in (0, 3) for j in place):
                make_far(place)

    def over_columns(body):
        def step(n, carry):
            body(n // 2, n % 2)
            return carry

        lax.fori_loop(0, 4, step, 0)

    def first_pass(shared, work, fresh=False):
        def body(ix, iy):
            numbers = [4 * ix + 2 * iy + level for level in range(2)]
            if fresh:
                totals = [[jnp.zeros((128, 128), F32)] * 2] * 2
            else:
                totals = [[sums[f, number] for f in range(2)] for number in numbers]

            def add(level, place, k, entry, product):
                number = numbers[level]
                volume, weighed = totals[level]
                square = jnp.maximum(product[:, 0:128], 1.0e-30)
                inside = jnp.maximum(2.0 - square * lax.rsqrt(square), 0.0)
                two = inside * inside
                picked = mask_ref[ix, iy, level, k].astype(F32)
                weight = base[place + (slice(3, 4),)] * picked
                smooth = two * two * (2.5 - inside)
                volume = volume + smooth
                smooth = smooth * weight
                weighed = weighed + smooth
                slope = two * inside * weight
                mass_w[number, entry] = smooth
                mass_g[number, entry] = slope
                mass_e[number, entry] = slope * product[:, 128:256]
                totals[level] = [volume, weighed]

            pair = near_terms[pl.ds(numbers[0], 2)].reshape(256, DEPTH)
            for low, high in zip(*(partners((ix, iy, level), shared) for level in range(2))):
                product = jnp.dot(pair, far_terms[low[0]], preferred_element_type=F32)
                add(0, *low, product[0:128])
                add(1, *high, product[128:256])
            for level, digit_list in work:
                for place, k, entry in partners((ix, iy, level), digit_list):
                    near = near_terms[numbers[level]]
                    product = jnp.dot(near, far_terms[place], preferred_element_type=F32)
                    add(level, place, k, entry, product)
            for level in range(2):
                for f in range(2):
                    sums[f, numbers[level]] = totals[level][f]

        over_columns(body)

    def second_pass(work, fresh=False):
        def body(ix, iy):
            for level, digit_list in work:
                leaf = (ix, iy, level)
                number = 4 * ix + 2 * iy + level
                if fresh:
                    volume = jnp.zeros((128, 128), F32)
                    spread = jnp.zeros((128, 128), F32)
                else:
                    volume = sums[2, number]
                    spread = sums[3, number]
                for place, k, entry in partners(leaf, digit_list):
                    weight = ratio[place + (slice(0, 1),)]
                    volume = volume + weight * mass_w[number, entry]
                    spread = spread + weight * mass_e[number, entry]
                sums[2, number] = volume
                sums[3, number] = spread

        over_columns(body)

    def third_pass(work, fresh=False):
        def body(ix, iy):
            for level, digit_list in work:
                leaf = (ix, iy, level)
                number = 4 * ix + 2 * iy + level
                if fresh:
                    totals = [jnp.zeros((128, 128), F32)] * 5
                else:
                    totals = [sums[f, number] for f in range(5)]
                for place, k, entry in partners(leaf, digit_list):
                    dense = far_columns[0, number] + state[place + (slice(0, 1),)]
                    sticky = far_columns[1, number] + state[place + (slice(1, 2),)]
                    damp = sticky * pltpu.reciprocal(dense, approx=True)
                    mine = far_columns[2, number] + damp
                    theirs = state[place + (slice(2, 3),)] + damp
                    push = mass_g[number, entry] * (mine + theirs)
                    totals[0] = totals[0] + push
                    for d in range(3):
                        totals[1 + d] = totals[1 + d] + push * placed[place + (slice(d, d + 1),)]
                    totals[4] = totals[4] + mass_e[number, entry] * mine
                for f in range(5):
                    sums[f, number] = totals[f]

        over_columns(body)

    lane = lax.broadcasted_iota(jnp.int32, (128, 128), 1)

    def gather(fields, numbers, fresh=False):
        packed = jnp.zeros((128, 128), F32) if fresh else pack[...]
        for f in fields:
            for number in numbers:
                total = jnp.sum(sums[f, number], axis=1, keepdims=True)
                packed = jnp.where(lane == 8 * f + number, total, packed)
        pack[...] = packed

    lower, upper = range(0, 8, 2), range(1, 8, 2)

    first_pass(INSIDE, [], fresh=True)
    for copy in first[UPWARD:]:
        copy.wait_recv()
    make_outer_far((1, 2, 3))
    first_pass(BESIDE, [(1, BEYOND)])
    for copy in first[:UPWARD]:
        copy.wait_recv()
    make_outer_far((0,))
    first_pass([], [(0, BEYOND)])

    gather((0, 1), range(8), fresh=True)
    table[...] = jnp.transpose(pack[...])
    mass = own[48:56, :]
    volume = 1.0 / (1.0 + 0.125 * table[0:8, :])
    summed_mass = mass + 0.125 * table[8:16, :]
    rated = volume / mass
    for number, (ix, iy, iz) in enumerate(LEAVES):
        ratio[1 + ix, 1 + iy, 1 + iz] = rated[number : number + 1, :]
    second = exchange(ratio, devices, send_sems.at[1], recv_sems.at[1], EVERY)

    def finish_state(numbers):
        gather((2, 3), numbers)
        table[...] = jnp.transpose(pack[...])
        density = summed_mass / (volume + 0.125 * table[16:24, :])
        sticky = jnp.maximum(1.25 * table[24:32, :], 0.0)
        specific = (2.0 / 3.0) * own[56:64, :] / density
        for number in numbers:
            place = tuple(1 + i for i in LEAVES[number])
            for f, rows in enumerate((density, sticky, specific)):
                row = rows[number : number + 1, :]
                state[place + (slice(f, f + 1),)] = row
                own[8 * f + number : 8 * f + number + 1, :] = row
            state[place + (slice(3, 4),)] = jnp.zeros((1, 128), F32)

    second_pass([(0, INSIDE), (1, INSIDE)], fresh=True)
    for copy in second[UPWARD:]:
        copy.wait_recv()
    second_pass([(0, BESIDE), (1, BESIDE + BEYOND)])
    finish_state(upper)
    third = exchange(state, devices, send_sems.at[2], recv_sems.at[2], EVERY[:UPWARD])
    for copy in second[:UPWARD]:
        copy.wait_recv()
    second_pass([(0, BEYOND)])
    finish_state(lower)
    third += exchange(state, devices, send_sems.at[2], recv_sems.at[2], EVERY[UPWARD:])

    turned = jnp.transpose(own[...])
    for f in range(3):
        for number in range(8):
            column = 8 * f + number
            far_columns[f, number] = jnp.broadcast_to(turned[:, column : column + 1], (128, 128))

    third_pass([(0, INSIDE), (1, INSIDE)], fresh=True)
    for copy in third[UPWARD:]:
        copy.wait_recv()
    third_pass([(0, BESIDE), (1, BESIDE + BEYOND)])
    gather(range(5), upper, fresh=True)
    for copy in third[:UPWARD]:
        copy.wait_recv()
    third_pass([(0, BEYOND)])
    gather(range(5), lower)
    table[...] = jnp.transpose(pack[...])

    for number, (ix, iy, iz) in enumerate(LEAVES):
        valid = own[64 + number : 65 + number, :] > 0.5
        total = table[number : number + 1, :]
        for d in range(3):
            row = 8 * (1 + d) + number
            spot = placed[1 + ix, 1 + iy, 1 + iz, d : d + 1, :]
            value = 1.25 * (spot * total - table[row : row + 1, :])
            accel_ref[ix, iy, d, iz : iz + 1, :] = jnp.where(valid, value, 0.0)
        rate_ref[ix, iy, iz : iz + 1, :] = jnp.where(
            valid, 1.25 * table[32 + number : 33 + number, :], 0.0
        )
    for copy in first + second + third:
        copy.wait_send()


def shards(offsets, velocity, mass, energy, partner_mask, counts):
    vmem = pl.BlockSpec(memory_space=pltpu.VMEM)
    smem = pl.BlockSpec(memory_space=pltpu.SMEM)
    offsets = jnp.transpose(offsets, (0, 1, 3, 2, 4))
    velocity = jnp.transpose(velocity, (0, 1, 3, 2, 4))
    acceleration, rate = pl.pallas_call(
        kernel,
        out_shape=(
            jax.ShapeDtypeStruct(offsets.shape, F32),
            jax.ShapeDtypeStruct(mass.shape, F32),
        ),
        in_specs=[vmem] * 4 + [smem] * 2,
        out_specs=(vmem, vmem),
        scratch_shapes=[
            pltpu.VMEM((4, 4, 4, 8, 128), F32),
            pltpu.VMEM((4, 4, 4, 8, 128), F32),
            pltpu.VMEM((4, 4, 4, 1, 128), F32),
            pltpu.VMEM((4, 4, 4, 4, 128), F32),
            pltpu.VMEM((128, 128), F32),
            pltpu.VMEM((8, 128, DEPTH), BF16),
            pltpu.VMEM((4, 4, 4, DEPTH, 256), BF16),
            pltpu.VMEM((3, 8, 128, 128), F32),
            pltpu.VMEM((5, 8, 128, 128), F32),
            pltpu.VMEM((8, 27, 128, 128), F32),
            pltpu.VMEM((8, 27, 128, 128), F32),
            pltpu.VMEM((8, 27, 128, 128), F32),
            pltpu.VMEM((128, 128), F32),
            pltpu.VMEM((128, 128), F32),
            pltpu.SemaphoreType.DMA((3, 26)),
            pltpu.SemaphoreType.DMA((3, 26)),
        ],
        compiler_params=pltpu.CompilerParams(
            collective_id=0,
            has_side_effects=True,
            vmem_limit_bytes=60 * 1024 * 1024,
        ),
    )(offsets, velocity, mass, energy, partner_mask, counts)
    return jnp.transpose(acceleration, (0, 1, 3, 2, 4)), rate


def solution(mesh):
    placed = (
        P("gx", "gy", "gz", None, None),
        P("gx", "gy", "gz", None, None),
        P("gx", "gy", "gz", None),
        P("gx", "gy", "gz", None),
        P("gx", "gy", "gz", None),
        P("gx", "gy", "gz"),
    )
    return jax.shard_map(
        shards,
        mesh=mesh,
        in_specs=placed,
        out_specs=(P("gx", "gy", "gz", None, None), P("gx", "gy", "gz", None)),
        check_vma=False,
    )
```

time: 76.4 us -> 63.6 us (0.83)
  Pallas kernels: 70.9 us -> 60.8 us
  local copies, waits for them, and re-layouts: 3.85 us -> 1.91 us
    pallas_call x1, Pallas kernels: 70.9 us -> 60.8 us  [shards(): pl.pallas_call(kernel, out_shape=(jax.ShapeDtypeStruct(offsets.shape, F32...]
    pallas_call x1 -> x0, local copies, waits for them, and re-layouts: 1.32 us -> none  [shards(): pl.pallas_call(kernel, out_shape=(jax.ShapeDtypeStruct(offsets.shape, F32...]
    unnamed x7 -> x4, local copies, waits for them, and re-layouts: 2.52 us -> 1.91 us
where the time goes in v2:
time: 63.6 us; the launch traced here: 63.3 us
  Pallas kernels  60.8 us (96%)
  local copies, waits for them, and re-layouts  1.91 us (3%)
  between operations  0.65 us (1%)
    pallas_call x1, Pallas kernels, shards(): pl.pallas_call(kernel, out_shape=(jax.ShapeDtypeStruct(offsets.shape, F32...  60.8 us
    unnamed x4, local copies, waits for them, and re-layouts  1.91 us

profile of v2, /device:TPU:1, one launch (start us, length us, event | category | flops | bytes accessed | tf_op | source)
XLA Modules:
  0.0 63.3 jit_solution(9392495878989097754)
XLA Ops:
  0.6 60.8 %shard_map.77 = (f32[2,2,3,2,128]{4,3,2,1,0:T(2,128)}, f32[2,2,2,128]{3,2,1,0:T(2,128)}) custom-call(f32[2,2,3,2,128]{4,3,2,1,0:T(2,128)} %bitcast.3, f32[2,2,3,2,128]{4,3,2,1,0:T(2,128)} %bitcast.4, f32[2,2,2,128]{3,2,1,0:T(2,128)} %mass_ref.1, f32[2,2,2,128]{3,2,1,0:T(2,128)} %energy_ref.1, s32[2,2,2,27]{3,2,1,0:T(2,128)} %mask_ref.1, s32[2,2,2]{2,1,0:T(2,128)} %counts_ref.1), custom_call_target="tpu_custom_call" | custom-call | tf_op jit(solution)/shard_map/pallas_call | solution.py:379
  61.4 0.0 copy-start
  61.4 1.3 %copy.10 = f32[2,2,2,3,128]{4,2,3,1,0:T(2,128)} copy(f32[2,2,2,3,128]{4,2,3,1,0:T(2,128)} %bitcast.5) | data formatting | bytes 24576
  62.7 0.0 copy-done
  62.7 0.6 copy.11
Async XLA Ops:
  61.4 1.3 %copy-start = (f32[2,2,2,128]{3,2,1,0:T(2,128)S(1)}, f32[2,2,2,128]{3,2,1,0:T(2,128)}, u32[]{:S(2)}) copy-start(f32[2,2,2,128]{3,2,1,0:T(2,128)} %get-tuple-element.9) | copy-start | bytes 12292

commit v3 on v2

--- a/solution.py
+++ b/solution.py
@@ -19,7 +19,7 @@
     if (dx, dy, dz) != (0, 0, 0)
 ]
 UPWARD = 9
-EVERY = range(len(DIRECTIONS))
+EVERY = sorted(range(len(DIRECTIONS)), key=lambda i: -abs(DIRECTIONS[i][0]) - abs(DIRECTIONS[i][1]))
 LEAVES = [(ix, iy, iz) for ix in range(2) for iy in range(2) for iz in range(2)]
 DIGITS = [(a, b, c) for a in range(3) for b in range(3) for c in range(3)]
 INSIDE = [d for d in DIGITS if max(d) < 2]
@@ -47,23 +47,22 @@
     return found
 
 
-def exchange(field, devices, send_sems, recv_sems, indices):
-    copies = []
+def exchange(field, devices, send_sem, recv_sems, indices):
     for index in indices:
         direction = DIRECTIONS[index]
-        copies.append(
-            pltpu.make_async_remote_copy(
-                src_ref=field.at[tuple(own_span(step) for step in direction)],
-                dst_ref=field.at[tuple(halo_span(step) for step in direction)],
-                send_sem=send_sems.at[index],
-                recv_sem=recv_sems.at[index],
-                device_id=devices[index],
-                device_id_type=MESH,
-            )
-        )
-    for copy in copies:
-        copy.start()
-    return copies
+        pltpu.make_async_remote_copy(
+            src_ref=field.at[tuple(own_span(step) for step in direction)],
+            dst_ref=field.at[tuple(halo_span(step) for step in direction)],
+            send_sem=send_sem,
+            recv_sem=recv_sems.at[0 if index < UPWARD else 1],
+            device_id=devices[index],
+            device_id_type=MESH,
+        ).start()
+
+
+def await_leaves(count, like, semaphore):
+    block = like.at[pl.ds(0, count)]
+    pltpu.make_async_copy(block, block, semaphore).wait()
 
 
 def partners(leaf, digit_list):
@@ -102,6 +101,9 @@
     mass_e,
     pack,
     table,
+    ghost_base,
+    ghost_ratio,
+    ghost_state,
     send_sems,
     recv_sems,
 ):
@@ -127,7 +129,7 @@
         own[64 + number : 65 + number, :] = valid.astype(F32)
 
     pl.semaphore_wait(barrier, len(DIRECTIONS))
-    first = exchange(base, devices, send_sems.at[0], recv_sems.at[0], EVERY)
+    exchange(base, devices, send_sems.at[0], recv_sems.at[0], EVERY)
 
     line = lax.broadcasted_iota(jnp.int32, (8, 128), 0)
 
@@ -294,12 +296,10 @@
     lower, upper = range(0, 8, 2), range(1, 8, 2)
 
     first_pass(INSIDE, [], fresh=True)
-    for copy in first[UPWARD:]:
-        copy.wait_recv()
+    await_leaves(40, ghost_base, recv_sems.at[0, 1])
     make_outer_far((1, 2, 3))
     first_pass(BESIDE, [(1, BEYOND)])
-    for copy in first[:UPWARD]:
-        copy.wait_recv()
+    await_leaves(16, ghost_base, recv_sems.at[0, 0])
     make_outer_far((0,))
     first_pass([], [(0, BEYOND)])
 
@@ -311,7 +311,7 @@
     rated = volume / mass
     for number, (ix, iy, iz) in enumerate(LEAVES):
         ratio[1 + ix, 1 + iy, 1 + iz] = rated[number : number + 1, :]
-    second = exchange(ratio, devices, send_sems.at[1], recv_sems.at[1], EVERY)
+    exchange(ratio, devices, send_sems.at[1], recv_sems.at[1], EVERY)
 
     def finish_state(numbers):
         gather((2, 3), numbers)
@@ -328,16 +328,14 @@
             state[place + (slice(3, 4),)] = jnp.zeros((1, 128), F32)
 
     second_pass([(0, INSIDE), (1, INSIDE)], fresh=True)
-    for copy in second[UPWARD:]:
-        copy.wait_recv()
+    await_leaves(40, ghost_ratio, recv_sems.at[1, 1])
     second_pass([(0, BESIDE), (1, BESIDE + BEYOND)])
     finish_state(upper)
-    third = exchange(state, devices, send_sems.at[2], recv_sems.at[2], EVERY[:UPWARD])
-    for copy in second[:UPWARD]:
-        copy.wait_recv()
+    exchange(state, devices, send_sems.at[2], recv_sems.at[2], [i for i in EVERY if i < UPWARD])
+    await_leaves(16, ghost_ratio, recv_sems.at[1, 0])
     second_pass([(0, BEYOND)])
     finish_state(lower)
-    third += exchange(state, devices, send_sems.at[2], recv_sems.at[2], EVERY[UPWARD:])
+    exchange(state, devices, send_sems.at[2], recv_sems.at[2], [i for i in EVERY if i >= UPWARD])
 
     turned = jnp.transpose(own[...])
     for f in range(3):
@@ -346,12 +344,10 @@
             far_columns[f, number] = jnp.broadcast_to(turned[:, column : column + 1], (128, 128))
 
     third_pass([(0, INSIDE), (1, INSIDE)], fresh=True)
-    for copy in third[UPWARD:]:
-        copy.wait_recv()
+    await_leaves(40, ghost_state, recv_sems.at[2, 1])
     third_pass([(0, BESIDE), (1, BESIDE + BEYOND)])
     gather(range(5), upper, fresh=True)
-    for copy in third[:UPWARD]:
-        copy.wait_recv()
+    await_leaves(16, ghost_state, recv_sems.at[2, 0])
     third_pass([(0, BEYOND)])
     gather(range(5), lower)
     table[...] = jnp.transpose(pack[...])
@@ -367,8 +363,8 @@
         rate_ref[ix, iy, iz : iz + 1, :] = jnp.where(
             valid, 1.25 * table[32 + number : 33 + number, :], 0.0
         )
-    for copy in first + second + third:
-        copy.wait_send()
+    for phase, like in enumerate((ghost_base, ghost_ratio, ghost_state)):
+        await_leaves(56, like, send_sems.at[phase])
 
 
 def shards(offsets, velocity, mass, energy, partner_mask, counts):
@@ -399,8 +395,11 @@
             pltpu.VMEM((8, 27, 128, 128), F32),
             pltpu.VMEM((128, 128), F32),
             pltpu.VMEM((128, 128), F32),
-            pltpu.SemaphoreType.DMA((3, 26)),
-            pltpu.SemaphoreType.DMA((3, 26)),
+            pltpu.VMEM((56, 8, 128), F32),
+            pltpu.VMEM((56, 1, 128), F32),
+            pltpu.VMEM((56, 4, 128), F32),
+            pltpu.SemaphoreType.DMA((3,)),
+            pltpu.SemaphoreType.DMA((3, 2)),
         ],
         compiler_params=pltpu.CompilerParams(
             collective_id=0,

time: 63.6 us -> 61.9 us (0.973)
  Pallas kernels: 60.8 us -> 58.9 us
    pallas_call x1, Pallas kernels: 60.8 us -> 58.9 us  [shards(): pl.pallas_call(kernel, out_shape=(jax.ShapeDtypeStruct(offsets.shape, F32...]
where the time goes in v3:
time: 61.9 us; the launch traced here: 61.5 us
  Pallas kernels  58.9 us (95%)
  local copies, waits for them, and re-layouts  1.91 us (3%)
  between operations  0.65 us (1%)
    pallas_call x1, Pallas kernels, shards(): pl.pallas_call(kernel, out_shape=(jax.ShapeDtypeStruct(offsets.shape, F32...  58.9 us
    unnamed x4, local copies, waits for them, and re-layouts  1.91 us

profile of v3, /device:TPU:1, one launch (start us, length us, event | category | flops | bytes accessed | tf_op | source)
XLA Modules:
  0.0 61.5 jit_solution(1318186233228418175)
XLA Ops:
  0.6 58.9 %shard_map.77 = (f32[2,2,3,2,128]{4,3,2,1,0:T(2,128)}, f32[2,2,2,128]{3,2,1,0:T(2,128)}) custom-call(f32[2,2,3,2,128]{4,3,2,1,0:T(2,128)} %bitcast.3, f32[2,2,3,2,128]{4,3,2,1,0:T(2,128)} %bitcast.4, f32[2,2,2,128]{3,2,1,0:T(2,128)} %mass_ref.1, f32[2,2,2,128]{3,2,1,0:T(2,128)} %energy_ref.1, s32[2,2,2,27]{3,2,1,0:T(2,128)} %mask_ref.1, s32[2,2,2]{2,1,0:T(2,128)} %counts_ref.1), custom_call_target="tpu_custom_call" | custom-call | tf_op jit(solution)/shard_map/pallas_call | solution.py:375
  59.6 0.0 copy-start
  59.6 1.3 %copy.10 = f32[2,2,2,3,128]{4,2,3,1,0:T(2,128)} copy(f32[2,2,2,3,128]{4,2,3,1,0:T(2,128)} %bitcast.5) | data formatting | bytes 24576
  60.9 0.0 copy-done
  60.9 0.6 copy.11
Async XLA Ops:
  59.6 1.3 %copy-start = (f32[2,2,2,128]{3,2,1,0:T(2,128)S(1)}, f32[2,2,2,128]{3,2,1,0:T(2,128)}, u32[]{:S(2)}) copy-start(f32[2,2,2,128]{3,2,1,0:T(2,128)} %get-tuple-element.9) | copy-start | bytes 12292
